TPU v7x, 128 devices: a whole 4x4x4 slice. The times are simulated.
128 devices in a mesh: rep: 2 (over core), seq: 64 (over y, x, z).
Axes of the slice: x: 4, y: 4, z: 4, core: 2. Of those that a mesh axis runs over, the one named last changes fastest.
Arguments:
- queries: bfloat16 [16384, 8192], P(('rep', 'seq')), parts along dimension 0, may hold values from -180 to 180
- keys: bfloat16 [65536, 1024], P(('rep', 'seq')), parts along dimension 0, may hold values from -6 to 6
- values: bfloat16 [65536, 1024], P(('rep', 'seq')), parts along dimension 0, may hold values from -6 to 6
- vertical: int32 [128, 64], P('rep'), parts along dimension 0, may hold values from 0 to 511, all different within a row
- vert_count: int32 [128], P('rep'), parts along dimension 0, may hold values from 1 to 64
- slash: int32 [128, 32], P('rep'), parts along dimension 0, may hold values from 0 to 383, all different within a row
- slash_count: int32 [128], P('rep'), parts along dimension 0, may hold values from 1 to 32
Outputs:
- attended: bfloat16 [16384, 8192], P(('rep', 'seq')), parts along dimension 0
There are 2 independent parts, one for each index of `rep`. A program takes and returns all parts, laid end to end along the dimension named above; each array names one. Nothing has to cross between parts.
Inputs may be any that keep to these rules, and one draw needn't show every extreme that they name: `vertical`: each row holds 64 different key block numbers; head h uses the first vert_count[h] of them. `slash`: each row holds 32 different numbers; head h uses the first slash_count[h] of them, each number s naming the slash offset s + 1 blocks.
All inputs are finite; a program needn't handle non-finite values.
Results may differ from a plain program's by a relative error of at most 0.007.
Values may be sent and summed in bfloat16 or wider, within the bound.
A program may use at most 128 MiB of HBM per device.

v0:
```python
import math

import jax
import jax.numpy as jnp
from jax import lax
from jax.sharding import PartitionSpec as P

QUERY_HEADS = 64
KV_HEADS = 8
HEAD_DIM = 128
BLOCK = 64
TURN = 4


def split_up(x, dim, count):
    shape = x.shape
    parts = x.reshape(*shape[:dim], count, shape[dim] // count, *shape[dim + 1 :])
    return jnp.moveaxis(parts, dim, 0)


def cut_rows(length, count):
    lap = length // count
    if lap >= 8:
        lap -= lap % 8
    return [lap * k for k in range(1, count)]


def joined_along(parts, dim):
    shape = list(parts.shape[1:])
    shape[dim] *= parts.shape[0]
    return jnp.moveaxis(parts, 0, dim).reshape(shape)


def cut_exchange(x, axis, pieces, split_dim, concat_dim):
    parts = split_up(x, split_dim, lax.axis_size(axis))
    cut = max(range(1, max(2, parts.ndim - 1)), key=lambda d: parts.shape[d])
    gathered = []
    for piece in jnp.split(parts, cut_rows(parts.shape[cut], pieces), axis=cut):
        if piece.size:
            gathered.append(lax.all_to_all(piece, axis, split_axis=0, concat_axis=0, tiled=True))
    return joined_along(jnp.concatenate(gathered, axis=cut), concat_dim)


def same_block(index):
    return index


def absorb(state, scores, valid, combine):
    peak, total, summed = state
    scores = jnp.where(valid, scores, -jnp.inf)
    new_peak = jnp.maximum(peak, jnp.max(scores, axis=1))
    factor = jnp.exp(peak - new_peak)
    weights = jnp.exp(scores - new_peak[:, None])
    total = total * factor + jnp.sum(weights, axis=1)
    summed = summed * factor[:, None] + combine(weights.astype(jnp.bfloat16))
    return (new_peak, total, summed)


def attend(
    query_blocks, storage, slot_of, head, first, stride, vertical, vert_count, slash, slash_count
):
    count_rows, block, width = query_blocks.shape
    total_blocks = storage.shape[0] // block
    cache = storage.reshape(total_blocks, block, 2 * width)
    scale = 1.0 / math.sqrt(width)
    rows = count_rows * block
    absolute = (
        total_blocks
        - count_rows * stride
        + first
        + stride * jnp.arange(count_rows, dtype=jnp.int32)
    )
    verticals = vertical[head]
    live_vert = vert_count[head]
    offsets = slash[head] + 1
    live_slash = slash_count[head]
    lanes = jnp.arange(TURN, dtype=jnp.int32)
    marks = jnp.arange(verticals.shape[0], dtype=jnp.int32) < live_vert
    flat_query = query_blocks.reshape(rows, width)
    diagonal = cache[slot_of(absolute)]
    scores = (
        jnp.einsum(
            "rqd,rkd->rqk", query_blocks, diagonal[:, :, :width], preferred_element_type=jnp.float32
        )
        * scale
    )
    causal = jnp.arange(block)[:, None] >= jnp.arange(block)[None, :]
    scores = jnp.where(causal[None], scores, -jnp.inf)
    peak = jnp.max(scores, axis=2)
    weights = jnp.exp(scores - peak[:, :, None])
    total = jnp.sum(weights, axis=2)
    summed = jnp.einsum(
        "rqk,rkd->rqd",
        weights.astype(jnp.bfloat16),
        diagonal[:, :, width:],
        preferred_element_type=jnp.float32,
    )
    state = (peak.reshape(rows), total.reshape(rows), summed.reshape(rows, width))

    def widen(usable):
        return jnp.broadcast_to(usable[:, None, :, None], (count_rows, block, TURN, block)).reshape(
            rows, TURN * block
        )

    def vertical_turn(step, state):
        picked = lax.dynamic_slice_in_dim(verticals, step * TURN, TURN)
        keys_here = cache[slot_of(picked)].reshape(TURN * block, 2 * width)
        scores = (
            lax.dot_general(
                flat_query,
                keys_here[:, :width],
                (((1,), (1,)), ((), ())),
                preferred_element_type=jnp.float32,
            )
            * scale
        )
        usable = (step * TURN + lanes < live_vert)[None, :] & (picked[None, :] < absolute[:, None])

        def combine(rounded):
            return jnp.dot(rounded, keys_here[:, width:], preferred_element_type=jnp.float32)

        return absorb(state, scores, widen(usable), combine)

    state = lax.fori_loop(0, (live_vert + TURN - 1) // TURN, vertical_turn, state)

    def slash_turn(step, state):
        picked = lax.dynamic_slice_in_dim(offsets, step * TURN, TURN)
        target = absolute[:, None] - picked[None, :]
        keys_here = cache[slot_of(target)].reshape(count_rows, TURN * block, 2 * width)
        scores = (
            jnp.einsum(
                "rqd,rkd->rqk",
                query_blocks,
                keys_here[:, :, :width],
                preferred_element_type=jnp.float32,
            ).reshape(rows, TURN * block)
            * scale
        )
        covered = jnp.any(
            (target[:, :, None] == verticals[None, None, :]) & marks[None, None, :], axis=2
        )
        usable = (step * TURN + lanes < live_slash)[None, :] & jnp.logical_not(covered)

        def combine(rounded):
            return jnp.einsum(
                "rqk,rkd->rqd",
                rounded.reshape(count_rows, block, TURN * block),
                keys_here[:, :, width:],
                preferred_element_type=jnp.float32,
            ).reshape(rows, width)

        return absorb(state, scores, widen(usable), combine)

    state = lax.fori_loop(0, (live_slash + TURN - 1) // TURN, slash_turn, state)
    peak, total, summed = state
    return (summed / total[:, None]).astype(jnp.bfloat16).reshape(count_rows, block, width)


def body(queries, keys, values, vertical, vert_count, slash, slash_count):
    seq_count = lax.axis_size("seq")
    position = lax.axis_index("seq")
    query_rows = queries.shape[0]
    key_rows = keys.shape[0]
    group_devices = seq_count // KV_HEADS
    local_cache = jnp.concatenate(
        [keys.reshape(key_rows, KV_HEADS, HEAD_DIM), values.reshape(key_rows, KV_HEADS, HEAD_DIM)],
        axis=2,
    )
    owners = jnp.arange(seq_count, dtype=jnp.int32) // group_devices
    sendable = jnp.take(local_cache, owners, axis=1)
    storage = cut_exchange(sendable, "seq", 2, 1, 0).reshape(seq_count * key_rows, 2 * HEAD_DIM)
    per_device = QUERY_HEADS // seq_count
    blocks = queries.reshape(query_rows // BLOCK, BLOCK, QUERY_HEADS, HEAD_DIM)
    gathered = lax.all_to_all(blocks, "seq", split_axis=2, concat_axis=0, tiled=True)
    results = [
        attend(
            gathered[:, :, 0, :],
            storage,
            same_block,
            position * per_device + 0,
            0,
            1,
            vertical,
            vert_count,
            slash,
            slash_count,
        )
    ]
    answer = lax.all_to_all(
        jnp.stack(results, axis=2), "seq", split_axis=0, concat_axis=2, tiled=True
    )
    return answer.reshape(query_rows, QUERY_HEADS * HEAD_DIM)


def solution(mesh):
    return jax.shard_map(
        body,
        mesh=mesh,
        in_specs=(
            P(("rep", "seq"), None),
            P(("rep", "seq"), None),
            P(("rep", "seq"), None),
            P("rep", None),
            P("rep"),
            P("rep", None),
            P("rep"),
        ),
        out_specs=P(("rep", "seq"), None),
        check_vma=False,
    )
```

profile of v0, /device:TPU:63, one launch (start us, length us, event | category | flops | bytes accessed | tf_op | source)
XLA Modules:
  0.0 1244.9 jit_solution(2181795530336012387)
XLA Ops:
  5.6 7.6 gather_fusion.2
  13.3 8.5 fusion.34
  21.8 4.2 slice_bitcast_fusion.1
  26.0 101.7 %all_to_all.40 = bf16[64,256,1,256]{3,1,2,0:T(8,128)(2,1)} all-to-all(bf16[64,256,1,256]{3,1,2,0:T(8,128)(2,1)S(1)} %get-tuple-element.273), channel_id=1, replica_groups=mesh['rep'=2,'seq'=64] {'seq'}, dimensions={0} | all-to-all | bytes 16777216 | tf_op jit(solution)/shard_map/all_to_all | solution.py:40
  127.7 10.8 all-to-all-start.1
  141.8 99.7 %all-to-all-done.1 = bf16[64,256,1,256]{3,1,2,0:T(8,128)(2,1)} async-done(((bf16[64,256,1,256]{3,1,2,0:T(8,128)(2,1)}), bf16[64,256,1,256]{3,1,2,0:T(8,128)(2,1)}, u32[]{:S(2)}, u32[]{:S(2)}) %all-to-all-start.1) | async-done | bytes 8388640 | tf_op jit(solution)/shard_map/all_to_all | solution.py:40
  241.5 20.5 %all-to-all-start.2 = ((bf16[2,64,64,128]{3,1,0,2:T(8,128)(2,1)}), bf16[2,64,64,128]{3,1,0,2:T(8,128)(2,1)S(1)}, u32[]{:S(2)}, u32[]{:S(2)}) async-start(bf16[2,64,64,128]{3,1,0,2:T(8,128)(2,1)} %copy.38), calls=%async_computation.2 | async-start | bytes 4194304 | tf_op jit(solution)/shard_map/all_to_all | solution.py:174
  265.0 13.6 %pad_maximum_fusion = bf16[64,512,1,256]{3,1,2,0:T(8,128)(2,1)} fusion(bf16[64,256,1,256]{3,1,2,0:T(8,128)(2,1)} %all-to-all-done.1, bf16[64,256,1,256]{3,1,2,0:T(8,128)(2,1)} %all_to_all.40), kind=kLoop, calls=%fused_computation.55 | loop fusion | flops 33554432 | bytes 33554432 | tf_op jit(solution)/shard_map/concatenate | solution.py:41
  278.6 8.5 gather_fusion.3
  294.7 69.6 %while.31 = (s32[]{:T(128)}, f32[8192]{0:T(1024)S(1)}, f32[8192]{0:T(1024)S(1)}, f32[8192,128]{1,0:T(8,128)}, s32[]{:T(128)}, /*index=5*/s32[]{:T(128)}, s32[64]...) while((s32[]{:T(128)}, f32[8192]{0:T(1024)S(1)}, ...), condition=%wide.region_5.6_spmd.clone, body=%wide.region_2.5_spmd.clone.sunk | while | flops 1090537600 | bytes 95295880 | solution.py:124
  295.8 6.3 gather_fusion.1
  306.2 11.8 reshape.350
  330.5 6.3 gather_fusion.1
  341.0 11.8 reshape.350
  364.3 100.6 %while.32 = (s32[]{:T(128)}, f32[8192]{0:T(1024)S(1)}, f32[8192]{0:T(1024)S(1)}, f32[8192,128]{1,0:T(8,128)}, s32[]{:T(128)}, /*index=5*/s32[]{:T(128)}, s32[32]...) while((s32[]{:T(128)}, f32[8192]{0:T(1024)S(1)}, ...), condition=%wide.region_10.11_spmd.clone.clone, body=%wide.region_6.10_spmd.clone.clone.sunk | while | flops 1099026688 | bytes 128866472 | solution.py:154
  366.4 19.7 %gather_fusion = bf16[512,64,256]{2,1,0:T(8,128)(2,1)} fusion(bf16[512,64,256]{2,1,0:T(8,128)(2,1)} %get-tuple-element.498, s32[1024]{0:T(1024)S(1)} %pad_clamp_fusion.7), kind=kCustom, calls=%fused_computation.1.clone.clone.1 | custom fusion | bytes 33556480 | tf_op jit(solution)/shard_map/while/body/gather | solution.py:129
  386.1 9.6 bitcast_reduce_fusion.2
  395.8 9.1 fusion.79
  409.2 5.4 bitcast_add_fusion.2
  416.7 19.7 %gather_fusion = bf16[512,64,256]{2,1,0:T(8,128)(2,1)} fusion(bf16[512,64,256]{2,1,0:T(8,128)(2,1)} %get-tuple-element.498, s32[1024]{0:T(1024)S(1)} %pad_clamp_fusion.7), kind=kCustom, calls=%fused_computation.1.clone.clone.1 | custom fusion | bytes 33556480 | tf_op jit(solution)/shard_map/while/body/gather | solution.py:129
  436.3 9.6 bitcast_reduce_fusion.2
  446.1 9.1 fusion.79
  459.5 5.4 bitcast_add_fusion.2
  467.8 772.6 %all_to_all.41 = bf16[128,64,1,128]{3,1,2,0:T(8,128)(2,1)S(1)} all-to-all(bf16[128,64,1,128]{3,1,2,0:T(8,128)(2,1)S(1)} %bitcast.112), channel_id=1, replica_groups=mesh['rep'=2,'seq'=64] {'seq'}, dimensions={0} | all-to-all | bytes 4194304 | tf_op jit(solution)/shard_map/all_to_all | solution.py:189
  (125 shorter events, 71.1 us)
Async XLA Ops:
  0.0 264.9 %copy-start = (s32[64,64]{1,0:T(8,128)S(1)}, s32[64,64]{1,0:T(8,128)}, u32[]{:S(2)}) copy-start(s32[64,64]{1,0:T(8,128)} %param.14) | copy-start | bytes 49156
  0.0 2.3 copy-start.9
  127.7 10.8 copy-start.8
  127.7 113.8 %all-to-all-start.1 = ((bf16[64,256,1,256]{3,1,2,0:T(8,128)(2,1)}), bf16[64,256,1,256]{3,1,2,0:T(8,128)(2,1)}, u32[]{:S(2)}, u32[]{:S(2)}) async-start(bf16[64,256,1,256]{3,1,2,0:T(8,128)(2,1)} %get-tuple-element.274), calls=%async_computation.1 | async-start | bytes 16777216 | tf_op jit(solution)/shard_map/all_to_all | solution.py:40
  139.1 122.9 %copy-start.11 = (s32[64]{0:T(128)S(1)}, s32[64]{0:T(128)}, u32[]{:S(2)}) copy-start(s32[64]{0:T(128)} %param.17) | copy-start | bytes 772
  139.1 124.2 %copy-start.12 = (s32[64]{0:T(128)S(1)}, s32[64]{0:T(128)}, u32[]{:S(2)}) copy-start(s32[64]{0:T(128)} %param.15) | copy-start | bytes 772
  139.2 125.6 %copy-start.10 = (s32[64,32]{0,1:T(8,128)S(1)}, s32[64,32]{0,1:T(8,128)}, u32[]{:S(2)}) copy-start(s32[64,32]{0,1:T(8,128)} %param.16) | copy-start | bytes 24580
  241.5 45.6 %all-to-all-start.2 = ((bf16[2,64,64,128]{3,1,0,2:T(8,128)(2,1)}), bf16[2,64,64,128]{3,1,0,2:T(8,128)(2,1)S(1)}, u32[]{:S(2)}, u32[]{:S(2)}) async-start(bf16[2,64,64,128]{3,1,0,2:T(8,128)(2,1)} %copy.38), calls=%async_computation.2 | async-start | bytes 4194304 | tf_op jit(solution)/shard_map/all_to_all | solution.py:174
  287.1 3.0 copy-start.7
  294.9 7.2 copy-start.5
  321.5 2.2 copy-start.2
  323.7 5.9 copy-start.6
  327.7 1.9 copy-start.3
  329.6 7.2 copy-start.5
  356.2 2.2 copy-start.2
  358.4 5.9 copy-start.6
  362.4 1.9 copy-start.3
  395.8 9.4 copy-start.4
  446.1 9.4 copy-start.4
  1240.4 4.5 copy-start.1
where the time goes:
time: 1250 us; the launch traced here: 1240 us
  blocking collectives  874 us (70%)
  local copies, waits for them, and re-layouts  125 us (10%)
  waiting for transfers between devices  99.7 us (8%)
  matrix products  58.2 us (5%)
  other arithmetic  54.3 us (4%)
  starting transfers between devices  31.3 us (3%)
    all_to_all x1, blocking collectives, body(): lax.all_to_all(jnp.stack(results, axis=2), 'seq', split_axis=0, concat_ax...  773 us
    all_to_all x1, blocking collectives, cut_exchange(): lax.all_to_all(piece, axis, split_axis=0, concat_axis=0, tiled=True)  102 us
    all_to_all x1, waiting for transfers between devices, cut_exchange(): lax.all_to_all(piece, axis, split_axis=0, concat_axis=0, tiled=True)  99.7 us
    gather x2, local copies, waits for them, and re-layouts, slash_turn(): cache[slot_of(target)].reshape(count_rows, TURN * block, 2 * width)  39.4 us
  transfers between devices with their start and end apart: 2, of which 1 were waited for; matrix products, arithmetic and copies ran while one was open for 2% of the time, Pallas kernels for 0%

commit v1 on v0

v1 whole, which is shorter than its diff:
```python
import functools, math
import jax, jax.numpy as jnp
from jax import lax
from jax.experimental import pallas as pl
from jax.experimental.pallas import tpu as pltpu
from jax.sharding import PartitionSpec as P

KV_HEADS = 8
HEAD_DIM = 128
D = HEAD_DIM
BLOCK = 64
VERT = 64
SLOTS=36
VT=8
ST=4
R=256
NEG=float("-inf")

def attn_kernel(sv, isv, offs, meta, qb, q_ref, kv_ref, o_ref, kvv, s_v, s_s, mx, acc, sm):
    h = pl.program_id(0)
    n_eff, n_full, ns = meta[0, h], meta[1, h], meta[2, h]
    vtiles = (n_eff + VT - 1) // VT
    ftiles = n_full // VT
    stiles = (ns + 1 + ST - 1) // ST
    c = math.log2(math.e) / math.sqrt(D)
    last = kv_ref.shape[0] // BLOCK - 1

    def gather(i, _):
        for u in range(VT):
            b = jnp.minimum(sv[h, i * VT + u], last)
            kvv[pl.ds((i * VT + u) * BLOCK, BLOCK), :] = kv_ref[pl.ds(b * BLOCK, BLOCK), :]
        return 0
    lax.fori_loop(0, vtiles, gather, 0)
    lane = lax.broadcasted_iota(jnp.int32, (1, 128), 1)
    low = lane < BLOCK
    nsub = R // BLOCK

    def two(x, y):
        return jnp.where(low, x, y)

    def row_tile(rt, _):
        q = q_ref[pl.ds(rt * R, R), :]
        blocks = [qb[rt * nsub + i] for i in range(nsub)]
        mx[...] = jnp.full_like(mx, NEG)

        def va(t, masked):
            k = kvv[pl.ds(t * VT * BLOCK, VT * BLOCK), 0:D]
            s = lax.dot_general(q, k, (((1,), (1,)), ((), ())), preferred_element_type=jnp.float32)
            if masked:
                ids = [sv[h, t * VT + u] for u in range(VT)]
                rows = []
                for i in range(nsub):
                    cols = []
                    for cg in range(VT // 2):
                        b = two(jnp.where(ids[2 * cg] < blocks[i], 0.0, NEG), jnp.where(ids[2 * cg + 1] < blocks[i], 0.0, NEG))
                        cols.append(s[i * BLOCK:(i + 1) * BLOCK, cg * 128:(cg + 1) * 128] + b)
                    rows.append(jnp.concatenate(cols, axis=1))
                s = jnp.concatenate(rows, axis=0)
            s_v[:, pl.ds(pl.multiple_of(t * VT * BLOCK, VT * BLOCK), VT * BLOCK)] = s
            m = s[:, 0:128]
            for cg in range(1, VT // 2):
                m = jnp.maximum(m, s[:, cg * 128:(cg + 1) * 128])
            mx[...] = jnp.maximum(mx[...], m)

        lax.fori_loop(0, ftiles, lambda t, _: (va(t, False), 0)[1], 0)
        lax.fori_loop(ftiles, vtiles, lambda t, _: (va(t, True), 0)[1], 0)

        def slots_of(t, i):
            return [blocks[i] - offs[h, t * ST + u] for u in range(ST)]

        def sa(t, first):
            for i in range(nsub):
                js = slots_of(t, i)
                k = jnp.concatenate([kv_ref[pl.ds(j * BLOCK, BLOCK), 0:D] for j in js], axis=0)
                s = lax.dot_general(q[i * BLOCK:(i + 1) * BLOCK], k, (((1,), (1,)), ((), ())), preferred_element_type=jnp.float32)
                m = mx[i * BLOCK:(i + 1) * BLOCK, :]
                for cg in range(ST // 2):
                    bias = []
                    for u in (2 * cg, 2 * cg + 1):
                        dead = jnp.where(t * ST + u <= ns, isv[h, js[u]], 1)
                        if first and u == 0:
                            dead = 0
                        bias.append(jnp.where(dead == 0, 0.0, NEG))
                    part = s[:, cg * 128:(cg + 1) * 128] + two(*bias)
                    if first and cg == 0:
                        ri = lax.broadcasted_iota(jnp.int32, (BLOCK, 128), 0)
                        ci = lax.broadcasted_iota(jnp.int32, (BLOCK, 128), 1)
                        part = jnp.where((ci >= BLOCK) | (ri >= ci), part, NEG)
                    s_s[i * BLOCK:(i + 1) * BLOCK, pl.ds(pl.multiple_of(t * ST * BLOCK + cg * 128, 128), 128)] = part
                    m = jnp.maximum(m, part)
                mx[i * BLOCK:(i + 1) * BLOCK, :] = m
        sa(0, True)
        lax.fori_loop(1, stiles, lambda t, _: (sa(t, False), 0)[1], 0)

        mrow = jnp.max(mx[...], axis=1, keepdims=True)
        mx[...] = jnp.broadcast_to(mrow * c, (R, 128))
        sm[...] = jnp.zeros_like(sm)
        acc[...] = jnp.zeros_like(acc)

        def vb(t, _):
            v = kvv[pl.ds(t * VT * BLOCK, VT * BLOCK), D:2 * D]
            mc = mx[...]
            ps = []
            tot = None
            for cg in range(VT // 2):
                s = s_v[:, pl.ds(pl.multiple_of(t * VT * BLOCK + cg * 128, 128), 128)]
                p = jnp.exp2(s * c - mc)
                tot = p if tot is None else tot + p
                ps.append(p.astype(jnp.bfloat16))
            sm[...] += tot
            acc[...] += jnp.dot(jnp.concatenate(ps, axis=1), v, preferred_element_type=jnp.float32)
            return 0
        lax.fori_loop(0, vtiles, vb, 0)

        def sb(t, _):
            for i in range(nsub):
                js = slots_of(t, i)
                rows = slice(i * BLOCK, (i + 1) * BLOCK)
                v = jnp.concatenate([kv_ref[pl.ds(j * BLOCK, BLOCK), D:2 * D] for j in js], axis=0)
                mc = mx[rows, :]
                ps = []
                tot = sm[rows, :]
                for cg in range(ST // 2):
                    s = s_s[rows, pl.ds(pl.multiple_of(t * ST * BLOCK + cg * 128, 128), 128)]
                    p = jnp.exp2(s * c - mc)
                    tot = tot + p
                    ps.append(p.astype(jnp.bfloat16))
                sm[rows, :] = tot
                acc[rows, :] += jnp.dot(jnp.concatenate(ps, axis=1), v, preferred_element_type=jnp.float32)
            return 0
        lax.fori_loop(0, stiles, sb, 0)
        total = jnp.sum(sm[...], axis=1, keepdims=True)
        o_ref[pl.ds(rt * R, R), :] = (acc[...] / total).astype(o_ref.dtype)
        return 0
    lax.fori_loop(0, q_ref.shape[0] // R, row_tile, 0)


def attend(tables, q, kv):
    rows, cols = q.shape
    heads = cols // D
    return pl.pallas_call(
        attn_kernel,
        grid_spec=pltpu.PrefetchScalarGridSpec(
            num_scalar_prefetch=5,
            grid=(heads,),
            in_specs=[pl.BlockSpec((rows, D), lambda h, *_: (0, h)),
                      pl.BlockSpec(memory_space=pltpu.VMEM)],
            out_specs=pl.BlockSpec((rows, D), lambda h, *_: (0, h)),
            scratch_shapes=[
                pltpu.VMEM((VERT * BLOCK, 2 * D), jnp.bfloat16),
                pltpu.VMEM((R, VERT * BLOCK), jnp.float32),
                pltpu.VMEM((R, SLOTS * BLOCK), jnp.float32),
                pltpu.VMEM((R, 128), jnp.float32),
                pltpu.VMEM((R, D), jnp.float32),
                pltpu.VMEM((R, 128), jnp.float32),
            ],
        ),
        out_shape=jax.ShapeDtypeStruct((rows, cols), jnp.bfloat16),
        compiler_params=pltpu.CompilerParams(vmem_limit_bytes=56 << 20),
    )(*tables, q, kv)


def tables_of(vertical, vert_count, slash, slash_count, blocks, context_blocks, query_blocks):
    n = vertical.shape[1]
    idx = jnp.arange(n, dtype=jnp.int32)
    live = idx[None] < vert_count[:, None]
    key = jnp.where(live, vertical, 4096 + idx[None])
    rank = jnp.sum((key[:, None, :] < key[:, :, None]).astype(jnp.int32), axis=2)
    sv = jnp.sum(jnp.where(rank[:, :, None] == idx[None, None, :], key[:, :, None], 0), axis=1)
    n_eff = jnp.sum((key < jnp.max(blocks)).astype(jnp.int32), axis=1)
    n_full = jnp.sum((key < jnp.min(blocks)).astype(jnp.int32), axis=1)
    isv = jnp.sum((key[:, :, None] == jnp.arange(context_blocks, dtype=jnp.int32)[None, None]).astype(jnp.int32), axis=1)
    offs = jnp.pad(slash + 1, ((0, 0), (1, SLOTS - 1 - slash.shape[1])))
    meta = jnp.stack([n_eff, n_full, slash_count])
    return sv, isv, offs, meta, blocks


MESH_ID = pl.DeviceIdType.MESH
PEERS = 8
LATE = (5, 6, 7)


def place():
    rep = lax.axis_index("rep")
    seq = lax.axis_index("seq")
    y, x, z = seq // 16, (seq // 4) % 4, seq % 4
    ring = y * (1 - rep) + z * rep
    other = z * (1 - rep) + y * rep
    shifted = (x + rep) % 4
    half, low = shifted // 2, shifted % 2
    return rep, seq, ring, half, low, other


def seq_at(rep, ring, half, low, other):
    y = ring * (1 - rep) + other * rep
    z = other * (1 - rep) + ring * rep
    x = (2 * half + low + 4 - rep) % 4
    return y * 16 + x * 4 + z


def peer_seq(rep, ring, turn, group):
    half, other = group // 4, group % 4
    return seq_at(rep, ring, half, (turn + half) % 2, other)


def aligned(index, size):
    return pl.ds(pl.multiple_of(index * size, size), size)


def spread_kernel(keys, values, queries, kv, q_out, local_sem, first_send, first_recv, tree_send, tree_recv):
    rep, seq, ring, half, low, other = place()
    group = half * 4 + other
    turn = (low + half) % 2
    rows = keys.shape[0]
    q_rows = queries.shape[0]
    q_width = q_out.shape[1]

    peers = [(rep, peer_seq(rep, ring, turn, (group + d) % PEERS)) for d in range(1, PEERS)]
    neighbours = {
        "pair": (rep, seq_at(rep, ring, half, 1 - low, other)),
        "up": (rep, seq_at(rep, (ring + 1) % 4, half, low, other)),
        "down": (rep, seq_at(rep, (ring + 3) % 4, half, low, other)),
    }
    barrier = pltpu.get_barrier_semaphore()
    for device in peers + list(neighbours.values()):
        pl.semaphore_signal(barrier, inc=1, device_id=device, device_id_type=MESH_ID)
    pl.semaphore_wait(barrier, len(peers) + len(neighbours))

    def first(d, kind):
        to = (group + d) % PEERS
        source = keys if kind == 0 else values
        return pltpu.make_async_remote_copy(
            src_ref=source.at[:, aligned(to, HEAD_DIM)],
            dst_ref=kv.at[aligned(seq, rows), pl.ds(kind * HEAD_DIM, HEAD_DIM)],
            send_sem=first_send.at[d, kind],
            recv_sem=first_recv.at[d, kind],
            device_id=peers[d - 1],
            device_id_type=MESH_ID,
        )

    def first_q(d):
        to = (group + d) % PEERS
        return pltpu.make_async_remote_copy(
            src_ref=queries.at[:, aligned(to, q_width)],
            dst_ref=q_out.at[aligned(group, q_rows), :],
            send_sem=first_send.at[d, 2],
            recv_sem=first_recv.at[d, 2],
            device_id=peers[d - 1],
            device_id_type=MESH_ID,
        )

    own = [
        pltpu.make_async_copy(keys.at[:, aligned(group, HEAD_DIM)], kv.at[aligned(seq, rows), pl.ds(0, HEAD_DIM)], local_sem.at[0]),
        pltpu.make_async_copy(values.at[:, aligned(group, HEAD_DIM)], kv.at[aligned(seq, rows), pl.ds(HEAD_DIM, HEAD_DIM)], local_sem.at[1]),
        pltpu.make_async_copy(queries.at[:, aligned(group, q_width)], q_out.at[aligned(group, q_rows), :], local_sem.at[2]),
    ]
    own[0].start()
    own[1].start()
    for d in range(1, PEERS):
        first(d, 0).start()
        first(d, 1).start()
    own[2].start()
    for d in range(1, PEERS):
        first_q(d).start()

    def piece_rows(up, flip, d):
        origin_low = (low + flip) % 2
        origin_turn = (origin_low + half) % 2
        origin_ring = (ring + 4 - up) % 4
        return aligned(peer_seq(rep, origin_ring, origin_turn, (group + PEERS - d) % PEERS), rows)

    moves = {"pair": (0, 1), "up": (1, 0), "down": (3, 0)}
    sends = []

    def pass_on(up, flip, d, way):
        step_up, step_flip = moves[way]
        at = piece_rows(up, flip, d)
        copy = pltpu.make_async_remote_copy(
            src_ref=kv.at[at, :],
            dst_ref=kv.at[at, :],
            send_sem=tree_send.at[len(sends)],
            recv_sem=tree_recv.at[(up + step_up) % 4, (flip + step_flip) % 2, d],
            device_id=neighbours[way],
            device_id_type=MESH_ID,
        )
        copy.start()
        sends.append(copy)

    def arrived(up, flip, d):
        at = piece_rows(up, flip, d)
        pltpu.make_async_remote_copy(
            src_ref=kv.at[at, :],
            dst_ref=kv.at[at, :],
            send_sem=tree_send.at[0],
            recv_sem=tree_recv.at[up, flip, d],
            device_id=neighbours["pair"],
            device_id_type=MESH_ID,
        ).wait_recv()

    actions = []
    for d in range(PEERS):
        onward = "up" if d % 2 == 0 else "down"
        turning = 1 if d % 2 == 0 else 3
        late = d in LATE
        actions.append((d, 0, 0, d, ["up", "down", "pair"]))
        for up in (1, 3):
            ways = [onward] if up == turning else []
            actions.append((d + 1, up, 0, d, ways + (["pair"] if late else [])))
            actions.append((d + 2, up, 1, d, [] if late else ways))
        actions.append((d + 2, 2, 0, d, ["pair"] if late else []))
        actions.append((d + 1, 0, 1, d, [] if late else ["up", "down"]))
        actions.append((d + 3, 2, 1, d, []))
    ends = [a for a in actions if not a[4]]
    for _, up, flip, d, ways in sorted(a for a in actions if a[4]):
        if (up, flip) != (0, 0):
            arrived(up, flip, d)
        elif d == 0:
            own[0].wait()
            own[1].wait()
        else:
            first(d, 0).wait_recv()
            first(d, 1).wait_recv()
        for way in ways:
            pass_on(up, flip, d, way)
    for _, up, flip, d, _ in ends:
        arrived(up, flip, d)
    own[2].wait()
    for d in range(1, PEERS):
        first_q(d).wait_recv()
    for d in range(1, PEERS):
        first(d, 0).wait_send()
        first(d, 1).wait_send()
        first_q(d).wait_send()
    for copy in sends:
        copy.wait_send()


def spread(keys, values, queries):
    seq_count = lax.axis_size("seq")
    any_space = pl.BlockSpec(memory_space=pl.ANY)
    return pl.pallas_call(
        spread_kernel,
        out_shape=(
            jax.ShapeDtypeStruct((seq_count * keys.shape[0], 2 * HEAD_DIM), keys.dtype),
            jax.ShapeDtypeStruct((PEERS * queries.shape[0], queries.shape[1] // PEERS), queries.dtype),
        ),
        in_specs=[any_space] * 3,
        out_specs=(any_space, any_space),
        scratch_shapes=[
            pltpu.SemaphoreType.DMA((3,)),
            pltpu.SemaphoreType.DMA((PEERS, 3)),
            pltpu.SemaphoreType.DMA((PEERS, 3)),
            pltpu.SemaphoreType.DMA((56,)),
            pltpu.SemaphoreType.DMA((4, 2, PEERS)),
        ],
        compiler_params=pltpu.CompilerParams(collective_id=0, has_side_effects=True),
        name="spread",
    )(keys, values, queries)


def give_back_kernel(result, out, local_sem, send_sem, recv_sem):
    rep, seq, ring, half, low, other = place()
    group = half * 4 + other
    turn = (low + half) % 2
    rows, width = out.shape[0], result.shape[1]
    peers = [(rep, peer_seq(rep, ring, turn, (group + d) % PEERS)) for d in range(1, PEERS)]
    barrier = pltpu.get_barrier_semaphore()
    for device in peers:
        pl.semaphore_signal(barrier, inc=1, device_id=device, device_id_type=MESH_ID)
    pl.semaphore_wait(barrier, len(peers))
    copies = []
    for d in range(1, PEERS):
        copy = pltpu.make_async_remote_copy(
            src_ref=result.at[aligned((group + d) % PEERS, rows), :],
            dst_ref=out.at[:, aligned(group, width)],
            send_sem=send_sem.at[d],
            recv_sem=recv_sem.at[d],
            device_id=peers[d - 1],
            device_id_type=MESH_ID,
        )
        copy.start()
        copies.append(copy)
    own = pltpu.make_async_copy(result.at[aligned(group, rows), :], out.at[:, aligned(group, width)], local_sem)
    own.start()
    own.wait()
    for d in range(1, PEERS):
        pltpu.make_async_remote_copy(
            src_ref=result.at[aligned((group + d) % PEERS, rows), :],
            dst_ref=out.at[:, aligned((group + PEERS - d) % PEERS, width)],
            send_sem=send_sem.at[d],
            recv_sem=recv_sem.at[d],
            device_id=peers[d - 1],
            device_id_type=MESH_ID,
        ).wait_recv()
    for copy in copies:
        copy.wait_send()


def give_back(result, rows):
    any_space = pl.BlockSpec(memory_space=pl.ANY)
    return pl.pallas_call(
        give_back_kernel,
        out_shape=jax.ShapeDtypeStruct((rows, PEERS * result.shape[1]), result.dtype),
        in_specs=[any_space],
        out_specs=any_space,
        scratch_shapes=[
            pltpu.SemaphoreType.DMA,
            pltpu.SemaphoreType.DMA((PEERS,)),
            pltpu.SemaphoreType.DMA((PEERS,)),
        ],
        compiler_params=pltpu.CompilerParams(collective_id=1, has_side_effects=True),
        name="give_back",
    )(result)


def body(queries, keys, values, vertical, vert_count, slash, slash_count):
    rep, seq, ring, half, low, other = place()
    group = half * 4 + other
    turn = (low + half) % 2
    query_rows = queries.shape[0]
    per_device = query_rows // BLOCK
    seq_count = lax.axis_size("seq")
    context_blocks = seq_count * keys.shape[0] // BLOCK
    stretch_blocks = seq_count * per_device
    sources = peer_seq(rep, ring, turn, jnp.arange(PEERS, dtype=jnp.int32))
    blocks = (context_blocks - stretch_blocks + per_device * sources[:, None] + jnp.arange(per_device, dtype=jnp.int32)[None]).reshape(-1)
    per_group = vertical.shape[0] // KV_HEADS

    def mine(x):
        return lax.dynamic_slice_in_dim(x, group * per_group, per_group, 0)

    tables = tables_of(mine(vertical), mine(vert_count), mine(slash), mine(slash_count), blocks, context_blocks, stretch_blocks)
    kv, q = spread(keys, values, queries)
    return give_back(attend(tables, q, kv), query_rows)


def solution(mesh):
    return jax.shard_map(
        body,
        mesh=mesh,
        in_specs=(
            P(("rep", "seq"), None),
            P(("rep", "seq"), None),
            P(("rep", "seq"), None),
            P("rep", None),
            P("rep"),
            P("rep", None),
            P("rep"),
        ),
        out_specs=P(("rep", "seq"), None),
        check_vma=False,
    )
```

time: 1250 us -> 315 us (0.25)
  blocking collectives: 874 us -> 0 us
  Pallas kernels: 0 us -> 303 us
  local copies, waits for them, and re-layouts: 125 us -> 5.97 us
  waiting for transfers between devices: 99.7 us -> 0 us
  matrix products: 58.2 us -> 0 us
  other arithmetic: 54.3 us -> 5.59 us
  starting transfers between devices: 31.3 us -> 0 us
    all_to_all x2 -> x0, blocking collectives: 874 us -> none  [the longest x1 773 us: body(): lax.all_to_all(jnp.stack(results, axis=2), 'seq', split_axis=0, concat_ax...]
    pallas_call x0 -> x3, Pallas kernels: none -> 303 us  [the longest x1 133 us: attend(): pl.pallas_call(attn_kernel, grid_spec=pltpu.PrefetchScalarGridSpec(num_sc...]
    all_to_all x2 -> x0, waiting for transfers between devices: 99.7 us -> none  [the longest x1 99.7 us: cut_exchange(): lax.all_to_all(piece, axis, split_axis=0, concat_axis=0, tiled=True)]
    gather x6 -> x0, local copies, waits for them, and re-layouts: 68.1 us -> none  [the longest x2 39.4 us: slash_turn(): cache[slot_of(target)].reshape(count_rows, TURN * block, 2 * width)]
    dot_general x10 -> x0, matrix products: 58.2 us -> none  [the longest x2 19.2 us: slash_turn(): jnp.einsum('rqd,rkd->rqk', query_blocks, keys_here[:, :, :width], preferr...]
    all_to_all x2 -> x0, starting transfers between devices: 31.3 us -> none  [the longest x1 20.5 us: body(): lax.all_to_all(blocks, 'seq', split_axis=2, concat_axis=0, tiled=True)]
    reshape x7 -> x0, local copies, waits for them, and re-layouts: 28.4 us -> none  [the longest x2 23.6 us: widen(): jnp.broadcast_to(usable[:, None, :, None], (count_rows, block, TURN, block))]
    concatenate x2 -> x0, other arithmetic: 15 us -> none  [the longest x1 13.6 us: cut_exchange(): return joined_along(jnp.concatenate(gathered, axis=cut), concat_dim)]
  transfers between devices with their start and end apart: 2 -> 0, of which waited for: 1 -> 0; matrix products, arithmetic and copies ran while one was open for 2% -> 0% of each run, Pallas kernels for 0% -> 0%
where the time goes in v1:
time: 315 us
  Pallas kernels  303 us (96%)
  local copies, waits for them, and re-layouts  5.97 us (2%)
  other arithmetic  5.59 us (2%)
    pallas_call x1, Pallas kernels, attend(): pl.pallas_call(attn_kernel, grid_spec=pltpu.PrefetchScalarGridSpec(num_sc...  133 us
    pallas_call x1, Pallas kernels, spread(): pl.pallas_call(spread_kernel, out_shape=(jax.ShapeDtypeStruct((seq_count...  105 us
    pallas_call x1, Pallas kernels, give_back(): pl.pallas_call(give_back_kernel, out_shape=jax.ShapeDtypeStruct((rows, PE...  65.5 us

profile of v1, /device:TPU:63, one launch (start us, length us, event | category | flops | bytes accessed | tf_op | source)
XLA Modules:
  0.0 315.0 jit_solution(4877180655314492337)
XLA Ops:
  0.0 0.0 copy-start
  0.0 0.7 dynamic_slice.12
  0.8 0.7 dynamic-slice_bitcast_fusion
  1.5 0.8 fusion.1
  2.3 0.6 add.209.qb
  2.9 2.2 convert_reduce_fusion.3
  5.1 0.6 pad_add_fusion.meta
  5.7 0.3 convert_reduce_fusion.1
  6.0 0.8 select_reduce_fusion.sv
  6.9 0.8 convert_reduce_fusion.isv
  7.7 0.0 copy-done
  7.7 0.1 constant_dynamic-slice_fusion
  7.7 0.1 copy.11
  7.8 0.7 pad.4.offs
  8.5 105.3 %spread.1 = (bf16[32768,256]{1,0:T(8,128)(2,1)}, bf16[1024,1024]{1,0:T(8,128)(2,1)}) custom-call(bf16[512,1024]{1,0:T(8,128)(2,1)} %keys.1, bf16[512,1024]{1,0:T(8,128)(2,1)} %values.1, bf16[128,8192]{1,0:T(8,128)(2,1)} %queries.1), custom_call_target="tpu_custom_call" | custom-call | tf_op jit(solution)/shard_map/spread/pallas_call | solution.py:341
  113.8 132.6 %shard_map.73.result = bf16[1024,1024]{1,0:T(8,128)(2,1)} custom-call(s32[8,64]{1,0:T(8,128)} %select_reduce_fusion.sv, s32[8,512]{1,0:T(8,128)} %convert_reduce_fusion.isv, s32[8,36]{1,0:T(8,128)} %pad.4.offs, s32[3,8]{1,0:T(4,128)} %pad_add_fusion.meta, s32[16]{0:T(128)} %add.209.qb, bf16[1024,1024]{1,0:T(8,128)(2,1)} %get-tuple-element.7.q_ref, ...), custom_call_target="tpu_custom_call" | custom-call | tf_op jit(solution)/shard_map/pallas_call | solution.py:141
  246.4 65.5 %give_back.1 = bf16[128,8192]{1,0:T(8,128)(2,1)} custom-call(bf16[1024,1024]{1,0:T(8,128)(2,1)} %shard_map.73.result), custom_call_target="tpu_custom_call" | custom-call | tf_op jit(solution)/shard_map/give_back/pallas_call | solution.py:401
  311.9 3.1 copy.13
  (3 shorter events, 0.0 us)
Async XLA Ops:
  0.0 7.7 %copy-start = (s32[64,32]{0,1:T(8,128)S(1)}, s32[64,32]{0,1:T(8,128)}, u32[]{:S(2)}) copy-start(s32[64,32]{0,1:T(8,128)} %param.12) | copy-start | bytes 24580

commit v2 on v1

--- a/solution.py
+++ b/solution.py
@@ -10,17 +10,19 @@
 D = HEAD_DIM
 BLOCK = 64
 VERT = 64
-SLOTS=36
+SLOTS=40
 VT=8
 ST=4
-R=256
+R=1024
+SPANS = (4, 2, 1)
+FIRST = 2
+SLASH_SPANS = (4, 2, 1)
 NEG=float("-inf")
 
 def attn_kernel(sv, isv, offs, meta, qb, q_ref, kv_ref, o_ref, kvv, s_v, s_s, mx, acc, sm):
     h = pl.program_id(0)
-    n_eff, n_full, ns = meta[0, h], meta[1, h], meta[2, h]
+    n_eff, ns = meta[0, h], meta[1, h]
     vtiles = (n_eff + VT - 1) // VT
-    ftiles = n_full // VT
     stiles = (ns + 1 + ST - 1) // ST
     c = math.log2(math.e) / math.sqrt(D)
     last = kv_ref.shape[0] // BLOCK - 1
@@ -43,38 +45,44 @@
         blocks = [qb[rt * nsub + i] for i in range(nsub)]
         mx[...] = jnp.full_like(mx, NEG)
 
-        def va(t, masked):
-            k = kvv[pl.ds(t * VT * BLOCK, VT * BLOCK), 0:D]
-            s = lax.dot_general(q, k, (((1,), (1,)), ((), ())), preferred_element_type=jnp.float32)
-            if masked:
-                ids = [sv[h, t * VT + u] for u in range(VT)]
-                rows = []
-                for i in range(nsub):
-                    cols = []
-                    for cg in range(VT // 2):
-                        b = two(jnp.where(ids[2 * cg] < blocks[i], 0.0, NEG), jnp.where(ids[2 * cg + 1] < blocks[i], 0.0, NEG))
-                        cols.append(s[i * BLOCK:(i + 1) * BLOCK, cg * 128:(cg + 1) * 128] + b)
-                    rows.append(jnp.concatenate(cols, axis=1))
-                s = jnp.concatenate(rows, axis=0)
-            s_v[:, pl.ds(pl.multiple_of(t * VT * BLOCK, VT * BLOCK), VT * BLOCK)] = s
+        def va(t, span):
+            keys = span * VT * BLOCK
+            at = pl.ds(pl.multiple_of(t * VT * BLOCK, VT * BLOCK), keys)
+            s = lax.dot_general(q, kvv[at, 0:D], (((1,), (1,)), ((), ())), preferred_element_type=jnp.float32)
+            ids = [sv[h, t * VT + u] for u in range(span * VT)]
+            rows = []
+            for i in range(nsub):
+                cols = []
+                for cg in range(span * VT // 2):
+                    b = two(jnp.where(ids[2 * cg] < blocks[i], 0.0, NEG), jnp.where(ids[2 * cg + 1] < blocks[i], 0.0, NEG))
+                    cols.append(s[i * BLOCK:(i + 1) * BLOCK, cg * 128:(cg + 1) * 128] + b)
+                rows.append(jnp.concatenate(cols, axis=1))
+            s = jnp.concatenate(rows, axis=0)
+            s_v[:, at] = s
             m = s[:, 0:128]
-            for cg in range(1, VT // 2):
+            for cg in range(1, span * VT // 2):
                 m = jnp.maximum(m, s[:, cg * 128:(cg + 1) * 128])
             mx[...] = jnp.maximum(mx[...], m)
 
-        lax.fori_loop(0, ftiles, lambda t, _: (va(t, False), 0)[1], 0)
-        lax.fori_loop(ftiles, vtiles, lambda t, _: (va(t, True), 0)[1], 0)
-
-        def slots_of(t, i):
-            return [blocks[i] - offs[h, t * ST + u] for u in range(ST)]
-
-        def sa(t, first):
+        def over_tiles(step):
+            done = 0
+            for span in SPANS:
+                count = (vtiles - done) // span
+                lax.fori_loop(0, count, lambda n, _, done=done, span=span: (step(done + n * span, span), 0)[1], 0)
+                done = done + count * span
+
+        over_tiles(va)
+
+        def slots_of(t, i, span):
+            return [blocks[i] - offs[h, t * ST + u] for u in range(span * ST)]
+
+        def sa(t, span, first=False):
             for i in range(nsub):
-                js = slots_of(t, i)
+                js = slots_of(t, i, span)
                 k = jnp.concatenate([kv_ref[pl.ds(j * BLOCK, BLOCK), 0:D] for j in js], axis=0)
                 s = lax.dot_general(q[i * BLOCK:(i + 1) * BLOCK], k, (((1,), (1,)), ((), ())), preferred_element_type=jnp.float32)
                 m = mx[i * BLOCK:(i + 1) * BLOCK, :]
-                for cg in range(ST // 2):
+                for cg in range(span * ST // 2):
                     bias = []
                     for u in (2 * cg, 2 * cg + 1):
                         dead = jnp.where(t * ST + u <= ns, isv[h, js[u]], 1)
@@ -89,46 +97,54 @@
                     s_s[i * BLOCK:(i + 1) * BLOCK, pl.ds(pl.multiple_of(t * ST * BLOCK + cg * 128, 128), 128)] = part
                     m = jnp.maximum(m, part)
                 mx[i * BLOCK:(i + 1) * BLOCK, :] = m
-        sa(0, True)
-        lax.fori_loop(1, stiles, lambda t, _: (sa(t, False), 0)[1], 0)
+
+        def over_slots(step, done):
+            for span in SLASH_SPANS:
+                count = jnp.maximum(stiles - done, 0) // span
+                lax.fori_loop(0, count, lambda n, _, done=done, span=span: (step(done + n * span, span), 0)[1], 0)
+                done = done + count * span
+
+        sa(0, FIRST, True)
+        over_slots(sa, FIRST)
 
         mrow = jnp.max(mx[...], axis=1, keepdims=True)
         mx[...] = jnp.broadcast_to(mrow * c, (R, 128))
         sm[...] = jnp.zeros_like(sm)
         acc[...] = jnp.zeros_like(acc)
 
-        def vb(t, _):
-            v = kvv[pl.ds(t * VT * BLOCK, VT * BLOCK), D:2 * D]
+        def vb(t, span):
+            keys = span * VT * BLOCK
+            v = kvv[pl.ds(pl.multiple_of(t * VT * BLOCK, VT * BLOCK), keys), D:2 * D]
             mc = mx[...]
             ps = []
             tot = None
-            for cg in range(VT // 2):
+            for cg in range(keys // 128):
                 s = s_v[:, pl.ds(pl.multiple_of(t * VT * BLOCK + cg * 128, 128), 128)]
                 p = jnp.exp2(s * c - mc)
                 tot = p if tot is None else tot + p
                 ps.append(p.astype(jnp.bfloat16))
             sm[...] += tot
             acc[...] += jnp.dot(jnp.concatenate(ps, axis=1), v, preferred_element_type=jnp.float32)
-            return 0
-        lax.fori_loop(0, vtiles, vb, 0)
-
-        def sb(t, _):
+        over_tiles(vb)
+
+        def sb(t, span):
             for i in range(nsub):
-                js = slots_of(t, i)
+                js = slots_of(t, i, span)
                 rows = slice(i * BLOCK, (i + 1) * BLOCK)
                 v = jnp.concatenate([kv_ref[pl.ds(j * BLOCK, BLOCK), D:2 * D] for j in js], axis=0)
                 mc = mx[rows, :]
                 ps = []
                 tot = sm[rows, :]
-                for cg in range(ST // 2):
+                for cg in range(span * ST // 2):
                     s = s_s[rows, pl.ds(pl.multiple_of(t * ST * BLOCK + cg * 128, 128), 128)]
                     p = jnp.exp2(s * c - mc)
                     tot = tot + p
                     ps.append(p.astype(jnp.bfloat16))
                 sm[rows, :] = tot
                 acc[rows, :] += jnp.dot(jnp.concatenate(ps, axis=1), v, preferred_element_type=jnp.float32)
-            return 0
-        lax.fori_loop(0, stiles, sb, 0)
+
+        sb(0, FIRST)
+        over_slots(sb, FIRST)
         total = jnp.sum(sm[...], axis=1, keepdims=True)
         o_ref[pl.ds(rt * R, R), :] = (acc[...] / total).astype(o_ref.dtype)
         return 0
@@ -168,10 +184,9 @@
     rank = jnp.sum((key[:, None, :] < key[:, :, None]).astype(jnp.int32), axis=2)
     sv = jnp.sum(jnp.where(rank[:, :, None] == idx[None, None, :], key[:, :, None], 0), axis=1)
     n_eff = jnp.sum((key < jnp.max(blocks)).astype(jnp.int32), axis=1)
-    n_full = jnp.sum((key < jnp.min(blocks)).astype(jnp.int32), axis=1)
     isv = jnp.sum((key[:, :, None] == jnp.arange(context_blocks, dtype=jnp.int32)[None, None]).astype(jnp.int32), axis=1)
     offs = jnp.pad(slash + 1, ((0, 0), (1, SLOTS - 1 - slash.shape[1])))
-    meta = jnp.stack([n_eff, n_full, slash_count])
+    meta = jnp.stack([n_eff, slash_count])
     return sv, isv, offs, meta, blocks
 
 

time: 315 us -> 218 us (0.69)
  Pallas kernels: 303 us -> 207 us
    pallas_call x1, Pallas kernels: 133 us -> 64.7 us  [attend(): pl.pallas_call(attn_kernel, grid_spec=pltpu.PrefetchScalarGridSpec(num_sc...]
    pallas_call x1, Pallas kernels: 65.5 us -> 37.2 us  [give_back(): pl.pallas_call(give_back_kernel, out_shape=jax.ShapeDtypeStruct((rows, PE...]
where the time goes in v2:
time: 218 us
  Pallas kernels  207 us (95%)
  local copies, waits for them, and re-layouts  5.97 us (3%)
  other arithmetic  4.78 us (2%)
    pallas_call x1, Pallas kernels, spread(): pl.pallas_call(spread_kernel, out_shape=(jax.ShapeDtypeStruct((seq_count...  105 us
    pallas_call x1, Pallas kernels, attend(): pl.pallas_call(attn_kernel, grid_spec=pltpu.PrefetchScalarGridSpec(num_sc...  64.7 us
    pallas_call x1, Pallas kernels, give_back(): pl.pallas_call(give_back_kernel, out_shape=jax.ShapeDtypeStruct((rows, PE...  37.2 us

profile of v2, /device:TPU:63, one launch (start us, length us, event | category | flops | bytes accessed | tf_op | source)
XLA Modules:
  0.0 218.0 jit_solution(1045449821626654966)
XLA Ops:
  0.0 0.0 copy-start
  0.0 0.7 dynamic_slice.12
  0.8 0.7 dynamic-slice_bitcast_fusion
  1.5 0.7 iota_add_fusion
  2.2 0.6 add.208.qb
  2.8 1.5 convert_reduce_fusion.2
  4.3 0.6 pad_add_fusion.meta
  4.9 0.3 convert_reduce_fusion.1
  5.2 0.8 select_reduce_fusion.sv
  6.0 0.8 convert_reduce_fusion.isv
  6.8 0.0 copy-done
  6.8 0.1 constant_dynamic-slice_fusion
  6.9 0.1 copy.11
  7.0 0.7 pad.4.offs
  7.7 105.3 %spread.1 = (bf16[32768,256]{1,0:T(8,128)(2,1)}, bf16[1024,1024]{1,0:T(8,128)(2,1)}) custom-call(bf16[512,1024]{1,0:T(8,128)(2,1)} %keys.1, bf16[512,1024]{1,0:T(8,128)(2,1)} %values.1, bf16[128,8192]{1,0:T(8,128)(2,1)} %queries.1), custom_call_target="tpu_custom_call" | custom-call | tf_op jit(solution)/shard_map/spread/pallas_call | solution.py:356
  113.0 64.7 %shard_map.73.result = bf16[1024,1024]{1,0:T(8,128)(2,1)} custom-call(s32[8,64]{1,0:T(8,128)} %select_reduce_fusion.sv, s32[8,512]{1,0:T(8,128)} %convert_reduce_fusion.isv, s32[8,40]{1,0:T(8,128)} %pad.4.offs, s32[2,8]{1,0:T(2,128)} %pad_add_fusion.meta, s32[16]{0:T(128)} %add.208.qb, bf16[1024,1024]{1,0:T(8,128)(2,1)} %get-tuple-element.7.q_ref, ...), custom_call_target="tpu_custom_call" | custom-call | tf_op jit(solution)/shard_map/pallas_call | solution.py:157
  177.7 37.2 %give_back.1 = bf16[128,8192]{1,0:T(8,128)(2,1)} custom-call(bf16[1024,1024]{1,0:T(8,128)(2,1)} %shard_map.73.result), custom_call_target="tpu_custom_call" | custom-call | tf_op jit(solution)/shard_map/give_back/pallas_call | solution.py:416
  214.9 3.1 %copy.13 = bf16[128,8192]{1,0:T(8,128)(2,1)} copy(bf16[128,8192]{1,0:T(8,128)(2,1)} %give_back.1) | data formatting | bytes 4194304
  (3 shorter events, 0.0 us)
Async XLA Ops:
  0.0 6.8 %copy-start = (s32[64,32]{0,1:T(8,128)S(1)}, s32[64,32]{0,1:T(8,128)}, u32[]{:S(2)}) copy-start(s32[64,32]{0,1:T(8,128)} %param.12) | copy-start | bytes 24580

commit v3 on v2

--- a/solution.py
+++ b/solution.py
@@ -10,46 +10,89 @@
 D = HEAD_DIM
 BLOCK = 64
 VERT = 64
-SLOTS=40
-VT=8
-ST=4
-R=1024
+FAR = 1 << 20
+SLOTS = 40
+VT = 8
+ST = 4
+R = 1024
 SPANS = (4, 2, 1)
 FIRST = 2
 SLASH_SPANS = (4, 2, 1)
 NEG=float("-inf")
 
-def attn_kernel(sv, isv, offs, meta, qb, q_ref, kv_ref, o_ref, kvv, s_v, s_s, mx, acc, sm):
-    h = pl.program_id(0)
-    n_eff, ns = meta[0, h], meta[1, h]
-    vtiles = (n_eff + VT - 1) // VT
+MESH_ID = pl.DeviceIdType.MESH
+PEERS = 8
+LATE = (5, 7)
+
+
+def place():
+    rep = lax.axis_index("rep")
+    seq = lax.axis_index("seq")
+    y, x, z = seq // 16, (seq // 4) % 4, seq % 4
+    ring = y * (1 - rep) + z * rep
+    other = z * (1 - rep) + y * rep
+    shifted = (x + rep) % 4
+    half, low = shifted // 2, shifted % 2
+    return rep, seq, ring, half, low, other
+
+
+def seq_at(rep, ring, half, low, other):
+    y = ring * (1 - rep) + other * rep
+    z = other * (1 - rep) + ring * rep
+    x = (2 * half + low + 4 - rep) % 4
+    return y * 16 + x * 4 + z
+
+
+def peer_seq(rep, ring, turn, group):
+    half, other = group // 4, group % 4
+    return seq_at(rep, ring, half, (turn + half) % 2, other)
+
+
+def aligned(index, size):
+    return pl.ds(pl.multiple_of(index * size, size), size)
+
+
+def attn_kernel(first_block, vertical, vert_count, slash, slash_count, q_ref, kv_ref, o_ref, covered, kvv, s_v, s_s, mx, acc, sm):
+    rep, seq, ring, half, low, other = place()
+    h = (half * 4 + other) * pl.num_programs(0) + pl.program_id(0)
+    nv, ns = vert_count[h], slash_count[h]
+    vtiles = (nv + VT - 1) // VT
+    per_device = q_ref.shape[0] // BLOCK // PEERS
     stiles = (ns + 1 + ST - 1) // ST
     c = math.log2(math.e) / math.sqrt(D)
-    last = kv_ref.shape[0] // BLOCK - 1
+
+    @pl.when(pl.program_id(0) == 0)
+    def _():
+        def clear(i, _):
+            for u in range(8):
+                covered[i * 8 + u] = 0
+            return 0
+        lax.fori_loop(0, kv_ref.shape[0] // BLOCK // 8, clear, 0)
 
     def gather(i, _):
         for u in range(VT):
-            b = jnp.minimum(sv[h, i * VT + u], last)
+            b = vertical[h, i * VT + u]
+            covered[b] = jnp.where(i * VT + u < nv, 1, 0)
             kvv[pl.ds((i * VT + u) * BLOCK, BLOCK), :] = kv_ref[pl.ds(b * BLOCK, BLOCK), :]
         return 0
     lax.fori_loop(0, vtiles, gather, 0)
     lane = lax.broadcasted_iota(jnp.int32, (1, 128), 1)
-    low = lane < BLOCK
+    left = lane < BLOCK
     nsub = R // BLOCK
 
     def two(x, y):
-        return jnp.where(low, x, y)
+        return jnp.where(left, x, y)
 
     def row_tile(rt, _):
         q = q_ref[pl.ds(rt * R, R), :]
-        blocks = [qb[rt * nsub + i] for i in range(nsub)]
+        blocks = [first_block + per_device * peer_seq(rep, ring, (low + half) % 2, i // per_device) + i % per_device for i in range(nsub)]
         mx[...] = jnp.full_like(mx, NEG)
 
         def va(t, span):
             keys = span * VT * BLOCK
             at = pl.ds(pl.multiple_of(t * VT * BLOCK, VT * BLOCK), keys)
             s = lax.dot_general(q, kvv[at, 0:D], (((1,), (1,)), ((), ())), preferred_element_type=jnp.float32)
-            ids = [sv[h, t * VT + u] for u in range(span * VT)]
+            ids = [jnp.where(t * VT + u < nv, vertical[h, t * VT + u], FAR) for u in range(span * VT)]
             rows = []
             for i in range(nsub):
                 cols = []
@@ -73,19 +116,23 @@
 
         over_tiles(va)
 
-        def slots_of(t, i, span):
-            return [blocks[i] - offs[h, t * ST + u] for u in range(span * ST)]
+        def entry(k):
+            last = slash.shape[1] - 1
+            return min(k, last) if isinstance(k, int) else jnp.minimum(k, last)
+
+        def slots_of(t, i, span, own):
+            return [blocks[i] if own and u == 0 else blocks[i] - 1 - slash[h, entry(t * ST + u - 1)] for u in range(span * ST)]
 
         def sa(t, span, first=False):
             for i in range(nsub):
-                js = slots_of(t, i, span)
+                js = slots_of(t, i, span, first)
                 k = jnp.concatenate([kv_ref[pl.ds(j * BLOCK, BLOCK), 0:D] for j in js], axis=0)
                 s = lax.dot_general(q[i * BLOCK:(i + 1) * BLOCK], k, (((1,), (1,)), ((), ())), preferred_element_type=jnp.float32)
                 m = mx[i * BLOCK:(i + 1) * BLOCK, :]
                 for cg in range(span * ST // 2):
                     bias = []
                     for u in (2 * cg, 2 * cg + 1):
-                        dead = jnp.where(t * ST + u <= ns, isv[h, js[u]], 1)
+                        dead = jnp.where(t * ST + u <= ns, covered[js[u]], 1)
                         if first and u == 0:
                             dead = 0
                         bias.append(jnp.where(dead == 0, 0.0, NEG))
@@ -127,9 +174,9 @@
             acc[...] += jnp.dot(jnp.concatenate(ps, axis=1), v, preferred_element_type=jnp.float32)
         over_tiles(vb)
 
-        def sb(t, span):
+        def sb(t, span, first=False):
             for i in range(nsub):
-                js = slots_of(t, i, span)
+                js = slots_of(t, i, span, first)
                 rows = slice(i * BLOCK, (i + 1) * BLOCK)
                 v = jnp.concatenate([kv_ref[pl.ds(j * BLOCK, BLOCK), D:2 * D] for j in js], axis=0)
                 mc = mx[rows, :]
@@ -143,26 +190,33 @@
                 sm[rows, :] = tot
                 acc[rows, :] += jnp.dot(jnp.concatenate(ps, axis=1), v, preferred_element_type=jnp.float32)
 
-        sb(0, FIRST)
+        sb(0, FIRST, True)
         over_slots(sb, FIRST)
         total = jnp.sum(sm[...], axis=1, keepdims=True)
         o_ref[pl.ds(rt * R, R), :] = (acc[...] / total).astype(o_ref.dtype)
         return 0
     lax.fori_loop(0, q_ref.shape[0] // R, row_tile, 0)
 
-
-def attend(tables, q, kv):
+    def uncover(i, _):
+        for u in range(VT):
+            covered[vertical[h, i * VT + u]] = 0
+        return 0
+    lax.fori_loop(0, vtiles, uncover, 0)
+
+
+def attend(first_block, tables, q, kv):
     rows, cols = q.shape
     heads = cols // D
     return pl.pallas_call(
-        attn_kernel,
+        functools.partial(attn_kernel, first_block),
         grid_spec=pltpu.PrefetchScalarGridSpec(
-            num_scalar_prefetch=5,
+            num_scalar_prefetch=4,
             grid=(heads,),
             in_specs=[pl.BlockSpec((rows, D), lambda h, *_: (0, h)),
                       pl.BlockSpec(memory_space=pltpu.VMEM)],
             out_specs=pl.BlockSpec((rows, D), lambda h, *_: (0, h)),
             scratch_shapes=[
+                pltpu.SMEM((kv.shape[0] // BLOCK,), jnp.int32),
                 pltpu.VMEM((VERT * BLOCK, 2 * D), jnp.bfloat16),
                 pltpu.VMEM((R, VERT * BLOCK), jnp.float32),
                 pltpu.VMEM((R, SLOTS * BLOCK), jnp.float32),
@@ -174,52 +228,6 @@
         out_shape=jax.ShapeDtypeStruct((rows, cols), jnp.bfloat16),
         compiler_params=pltpu.CompilerParams(vmem_limit_bytes=56 << 20),
     )(*tables, q, kv)
-
-
-def tables_of(vertical, vert_count, slash, slash_count, blocks, context_blocks, query_blocks):
-    n = vertical.shape[1]
-    idx = jnp.arange(n, dtype=jnp.int32)
-    live = idx[None] < vert_count[:, None]
-    key = jnp.where(live, vertical, 4096 + idx[None])
-    rank = jnp.sum((key[:, None, :] < key[:, :, None]).astype(jnp.int32), axis=2)
-    sv = jnp.sum(jnp.where(rank[:, :, None] == idx[None, None, :], key[:, :, None], 0), axis=1)
-    n_eff = jnp.sum((key < jnp.max(blocks)).astype(jnp.int32), axis=1)
-    isv = jnp.sum((key[:, :, None] == jnp.arange(context_blocks, dtype=jnp.int32)[None, None]).astype(jnp.int32), axis=1)
-    offs = jnp.pad(slash + 1, ((0, 0), (1, SLOTS - 1 - slash.shape[1])))
-    meta = jnp.stack([n_eff, slash_count])
-    return sv, isv, offs, meta, blocks
-
-
-MESH_ID = pl.DeviceIdType.MESH
-PEERS = 8
-LATE = (5, 6, 7)
-
-
-def place():
-    rep = lax.axis_index("rep")
-    seq = lax.axis_index("seq")
-    y, x, z = seq // 16, (seq // 4) % 4, seq % 4
-    ring = y * (1 - rep) + z * rep
-    other = z * (1 - rep) + y * rep
-    shifted = (x + rep) % 4
-    half, low = shifted // 2, shifted % 2
-    return rep, seq, ring, half, low, other
-
-
-def seq_at(rep, ring, half, low, other):
-    y = ring * (1 - rep) + other * rep
-    z = other * (1 - rep) + ring * rep
-    x = (2 * half + low + 4 - rep) % 4
-    return y * 16 + x * 4 + z
-
-
-def peer_seq(rep, ring, turn, group):
-    half, other = group // 4, group % 4
-    return seq_at(rep, ring, half, (turn + half) % 2, other)
-
-
-def aligned(index, size):
-    return pl.ds(pl.multiple_of(index * size, size), size)
 
 
 def spread_kernel(keys, values, queries, kv, q_out, local_sem, first_send, first_recv, tree_send, tree_recv):
@@ -429,24 +437,11 @@
 
 
 def body(queries, keys, values, vertical, vert_count, slash, slash_count):
-    rep, seq, ring, half, low, other = place()
-    group = half * 4 + other
-    turn = (low + half) % 2
-    query_rows = queries.shape[0]
-    per_device = query_rows // BLOCK
     seq_count = lax.axis_size("seq")
     context_blocks = seq_count * keys.shape[0] // BLOCK
-    stretch_blocks = seq_count * per_device
-    sources = peer_seq(rep, ring, turn, jnp.arange(PEERS, dtype=jnp.int32))
-    blocks = (context_blocks - stretch_blocks + per_device * sources[:, None] + jnp.arange(per_device, dtype=jnp.int32)[None]).reshape(-1)
-    per_group = vertical.shape[0] // KV_HEADS
-
-    def mine(x):
-        return lax.dynamic_slice_in_dim(x, group * per_group, per_group, 0)
-
-    tables = tables_of(mine(vertical), mine(vert_count), mine(slash), mine(slash_count), blocks, context_blocks, stretch_blocks)
+    stretch_blocks = seq_count * queries.shape[0] // BLOCK
     kv, q = spread(keys, values, queries)
-    return give_back(attend(tables, q, kv), query_rows)
+    return give_back(attend(context_blocks - stretch_blocks, (vertical, vert_count, slash, slash_count), q, kv), queries.shape[0])
 
 
 def solution(mesh):

time: 218 us -> 207 us (0.950); the launches traced: 218 us -> 204 us
  Pallas kernels: 207 us -> 199 us
  other arithmetic: 4.78 us -> 0 us
    pallas_call x1, Pallas kernels: 37.2 us -> 23.6 us  [give_back(): pl.pallas_call(give_back_kernel, out_shape=jax.ShapeDtypeStruct((rows, PE...]
    pallas_call x1, Pallas kernels: 64.7 us -> 75.8 us  [attend(): pl.pallas_call(functools.partial(attn_kernel, first_block), grid_spec=plt...]
    pallas_call x1, Pallas kernels: 105 us -> 99.6 us  [spread(): pl.pallas_call(spread_kernel, out_shape=(jax.ShapeDtypeStruct((seq_count...]
    reduce_sum x4 -> x0, other arithmetic: 3.44 us -> none  [the longest x1 1.51 us: tables_of(): n_eff = jnp.sum((key < jnp.max(blocks)).astype(jnp.int32), axis=1)]
    unnamed x4 -> x2, local copies, waits for them, and re-layouts: 3.17 us -> 4.51 us
where the time goes in v3:
time: 207 us; the launch traced here: 204 us
  Pallas kernels  199 us (96%)
  local copies, waits for them, and re-layouts  4.51 us (2%)
    pallas_call x1, Pallas kernels, spread(): pl.pallas_call(spread_kernel, out_shape=(jax.ShapeDtypeStruct((seq_count...  99.6 us
    pallas_call x1, Pallas kernels, attend(): pl.pallas_call(functools.partial(attn_kernel, first_block), grid_spec=plt...  75.8 us
    pallas_call x1, Pallas kernels, give_back(): pl.pallas_call(give_back_kernel, out_shape=jax.ShapeDtypeStruct((rows, PE...  23.6 us
    unnamed x2, local copies, waits for them, and re-layouts  4.51 us

profile of v3, /device:TPU:63, one launch (start us, length us, event | category | flops | bytes accessed | tf_op | source)
XLA Modules:
  0.0 203.6 jit_solution(9007880980772616922)
XLA Ops:
  0.0 1.4 copy.8.slash
  1.4 99.6 %spread.1 = (bf16[32768,256]{1,0:T(8,128)(2,1)}, bf16[1024,1024]{1,0:T(8,128)(2,1)}) custom-call(bf16[512,1024]{1,0:T(8,128)(2,1)} %keys.1, bf16[512,1024]{1,0:T(8,128)(2,1)} %values.1, bf16[128,8192]{1,0:T(8,128)(2,1)} %queries.1), custom_call_target="tpu_custom_call" | custom-call | tf_op jit(solution)/shard_map/spread/pallas_call | solution.py:364
  101.1 75.8 %shard_map.73.result = bf16[1024,1024]{1,0:T(8,128)(2,1)} custom-call(s32[64,64]{1,0:T(8,128)} %vertical.1, s32[64]{0:T(128)} %vert_count.1, s32[64,32]{1,0:T(8,128)} %copy.8.slash, s32[64]{0:T(128)} %slash_count.1, bf16[1024,1024]{1,0:T(8,128)(2,1)} %get-tuple-element.7.q_ref, bf16[32768,256]{1,0:T(8,128)(2,1)} %get-tuple-element.8.kv_ref), custom_call_target="tpu_custom_call" | custom-call | tf_op jit(solution)/shard_map/pallas_call | solution.py:210
  176.8 23.6 %give_back.1 = bf16[128,8192]{1,0:T(8,128)(2,1)} custom-call(bf16[1024,1024]{1,0:T(8,128)(2,1)} %shard_map.73.result), custom_call_target="tpu_custom_call" | custom-call | tf_op jit(solution)/shard_map/give_back/pallas_call | solution.py:424
  200.5 3.1 %copy.10 = bf16[128,8192]{1,0:T(8,128)(2,1)} copy(bf16[128,8192]{1,0:T(8,128)(2,1)} %give_back.1) | data formatting | bytes 4194304

commit v4 on v3

--- a/solution.py
+++ b/solution.py
@@ -283,9 +283,6 @@
         first(d, 0).start()
         first(d, 1).start()
     own[2].start()
-    for d in range(1, PEERS):
-        first_q(d).start()
-
     def piece_rows(up, flip, d):
         origin_low = (low + flip) % 2
         origin_turn = (origin_low + half) % 2
@@ -345,6 +342,9 @@
             first(d, 1).wait_recv()
         for way in ways:
             pass_on(up, flip, d, way)
+        if (up, flip, d) == (0, 0, 0):
+            for to in range(1, PEERS):
+                first_q(to).start()
     for _, up, flip, d, _ in ends:
         arrived(up, flip, d)
     own[2].wait()

time: 207 us -> 209 us (level)
  the two profiles are of different devices: /device:TPU:63 before, /device:TPU:96 now
where the time goes in v4:
time: 209 us; the launch traced here: 212 us
  Pallas kernels  208 us (100%)
  local copies, waits for them, and re-layouts  4.51 us (2%)
    pallas_call x1, Pallas kernels, spread(): pl.pallas_call(spread_kernel, out_shape=(jax.ShapeDtypeStruct((seq_count...  100 us
    pallas_call x1, Pallas kernels, attend(): pl.pallas_call(functools.partial(attn_kernel, first_block), grid_spec=plt...  82.2 us
    pallas_call x1, Pallas kernels, give_back(): pl.pallas_call(give_back_kernel, out_shape=jax.ShapeDtypeStruct((rows, PE...  25.2 us
    unnamed x2, local copies, waits for them, and re-layouts  4.51 us

profile of v4, /device:TPU:96, one launch (start us, length us, event | category | flops | bytes accessed | tf_op | source)
XLA Modules:
  0.0 212.3 jit_solution(14161673106026612489)
XLA Ops:
  0.0 1.4 copy.8.slash
  1.4 100.4 %spread.1 = (bf16[32768,256]{1,0:T(8,128)(2,1)}, bf16[1024,1024]{1,0:T(8,128)(2,1)}) custom-call(bf16[512,1024]{1,0:T(8,128)(2,1)} %keys.1, bf16[512,1024]{1,0:T(8,128)(2,1)} %values.1, bf16[128,8192]{1,0:T(8,128)(2,1)} %queries.1), custom_call_target="tpu_custom_call" | custom-call | tf_op jit(solution)/shard_map/spread/pallas_call | solution.py:364
  101.8 82.2 %shard_map.73.result = bf16[1024,1024]{1,0:T(8,128)(2,1)} custom-call(s32[64,64]{1,0:T(8,128)} %vertical.1, s32[64]{0:T(128)} %vert_count.1, s32[64,32]{1,0:T(8,128)} %copy.8.slash, s32[64]{0:T(128)} %slash_count.1, bf16[1024,1024]{1,0:T(8,128)(2,1)} %get-tuple-element.7.q_ref, bf16[32768,256]{1,0:T(8,128)(2,1)} %get-tuple-element.8.kv_ref), custom_call_target="tpu_custom_call" | custom-call | tf_op jit(solution)/shard_map/pallas_call | solution.py:210
  184.1 25.2 %give_back.1 = bf16[128,8192]{1,0:T(8,128)(2,1)} custom-call(bf16[1024,1024]{1,0:T(8,128)(2,1)} %shard_map.73.result), custom_call_target="tpu_custom_call" | custom-call | tf_op jit(solution)/shard_map/give_back/pallas_call | solution.py:424
  209.2 3.1 %copy.10 = bf16[128,8192]{1,0:T(8,128)(2,1)} copy(bf16[128,8192]{1,0:T(8,128)(2,1)} %give_back.1) | data formatting | bytes 4194304
